TPU v7x, 256 devices: a whole 4x4x8 slice. The times are simulated.
256 devices in a mesh: grp: 8 (over y, core), tp: 16 (over z, x_hi), sec: 2 (over x_lo).
Axes of the slice: x: 4 (x_hi: 2, x_lo: 2; x = x_hi * 2 + x_lo), y: 4, z: 8, core: 2. Of those that a mesh axis runs over, the one named last changes fastest.
Arguments:
- layer_in: bfloat16 [2, 512, 4, 8192], P('sec', 'grp', None, 'tp'), may hold values from -6 to 6
- q_weight: bfloat16 [2, 8192, 8192], P('sec', 'grp', 'tp'), may hold values from -0.0625 to 0.0625
- kv_weight: bfloat16 [2, 8192, 2048], P('sec', 'grp', 'tp'), may hold values from -0.0625 to 0.0625
- o_weight: bfloat16 [2, 8192, 8192], P('sec', 'tp', 'grp'), may hold values from -0.5 to 0.5
- kv_cache: bfloat16 [2, 512, 4096, 256], P('sec', 'grp', 'tp'), may hold values from -600 to 600
- cache_lengths: int32 [512], P('grp'), may hold values from 1 to 512, as said below
- value_head: float32 [8192], P('tp'), may hold values from -0.0625 to 0.0625
Outputs:
- hidden_out: bfloat16 [2, 512, 4, 8192], P('sec', 'grp', None, 'tp')
- token_gap: float32 [512, 4], P('grp', 'sec')
Inputs may be any that keep to these rules, and one draw needn't show every extreme that they name: `cache_lengths`: every rollout has at least one cached position; some rollout fills the whole cache and some holds a single position. Positions at or after a rollout's length hold arbitrary values.
All inputs are finite; a program needn't handle non-finite values.
Results may differ from a plain program's by a relative error of at most 0.018.
Values may be sent and summed in bfloat16 or wider, within the bound.
A program may use at most 128 MiB of HBM per device.

v0:
```python
import jax
import jax.numpy as jnp
from jax import lax
from jax.sharding import PartitionSpec as P

KVH = 8
HD = 128
CACHE = 512


def from_partner(value, axis, bit):
    mask = 2**bit
    pairs = [(source, source ^ mask) for source in range(lax.axis_size(axis))]
    return lax.ppermute(value, axis, pairs)


def local(layer_in, q_weight, kv_weight, o_weight, kv_cache, cache_lengths, value_head):
    tp_count = lax.axis_size("tp")
    tp_place = lax.axis_index("tp")
    sec_count = lax.axis_size("sec")
    sec_place = lax.axis_index("sec")
    rollouts = layer_in.shape[1]
    new_steps = layer_in.shape[2]
    tokens = rollouts * new_steps
    local_in = layer_in[0].reshape(tokens, layer_in.shape[3])
    full_in = lax.all_gather(local_in, "tp", axis=1, tiled=True)
    query_local = q_weight[0]
    pair_local = kv_weight[0]

    def add_rows(piece):
        return jnp.dot(full_in, piece, preferred_element_type=jnp.float32)

    query_sum = add_rows(lax.all_gather(query_local, "grp", axis=0, tiled=True))
    pair_sum = add_rows(lax.all_gather(pair_local, "grp", axis=0, tiled=True))
    query_vals = query_sum.astype(jnp.bfloat16)
    pair_vals = pair_sum.astype(jnp.bfloat16)
    pair_size = max(tp_count // KVH, 1)
    is_even = tp_place % 2 == 0
    query_other, pair_other = from_partner((query_vals, pair_vals), "tp", 0)
    query_low = jnp.where(is_even, query_vals, query_other)
    query_high = jnp.where(is_even, query_other, query_vals)
    query_all = jnp.concatenate([query_low, query_high], axis=1)
    local_heads = 1
    new_key = jnp.where(is_even, pair_vals, pair_other).reshape(rollouts, new_steps, 1, HD)
    new_value = jnp.where(is_even, pair_other, pair_vals).reshape(rollouts, new_steps, 1, HD)
    groups = query_all.shape[1] // (local_heads * HD)
    query_five = query_all.reshape(rollouts, new_steps, local_heads, groups, HD)
    rows_dev = kv_cache.shape[2]
    span = rows_dev // local_heads
    start_pos = tp_place * rows_dev % CACHE
    cache_five = kv_cache[0].reshape(rollouts, local_heads, span, 2, HD)
    cache_keys = cache_five[:, :, :, 0, :]
    cache_vals = cache_five[:, :, :, 1, :]
    leader = tp_place % pair_size == 0
    visible = ((start_pos + jnp.arange(span))[None, :] < cache_lengths[:, None])[
        :, None, None, None, :
    ]
    causal = (jnp.arange(new_steps)[None, :] <= jnp.arange(new_steps)[:, None]) & leader
    causal = causal[None, :, None, None, :]
    score_scale = HD ** (-0.5)
    cache_scores = (
        jnp.einsum("rskgd,rkpd->rskgp", query_five, cache_keys, preferred_element_type=jnp.float32)
        * score_scale
    )
    new_scores = (
        jnp.einsum("rskgd,rtkd->rskgt", query_five, new_key, preferred_element_type=jnp.float32)
        * score_scale
    )
    row_peak = jnp.maximum(
        jnp.max(jnp.where(visible, cache_scores, -1e30), axis=-1),
        jnp.max(jnp.where(causal, new_scores, -1e30), axis=-1),
    )
    cache_w = jnp.where(visible, jnp.exp(cache_scores - row_peak[..., None]), 0.0)
    new_w = jnp.where(causal, jnp.exp(new_scores - row_peak[..., None]), 0.0)
    row_total = jnp.sum(cache_w, axis=-1) + jnp.sum(new_w, axis=-1)
    weighted = jnp.einsum(
        "rskgp,rkpd->rskgd",
        cache_w.astype(jnp.bfloat16),
        cache_vals,
        preferred_element_type=jnp.float32,
    )
    weighted = weighted + jnp.einsum(
        "rskgt,rtkd->rskgd",
        new_w.astype(jnp.bfloat16),
        new_value,
        preferred_element_type=jnp.float32,
    )
    own_heads = groups // 2
    low_part = (
        row_peak[:, :, :, :own_heads],
        row_total[:, :, :, :own_heads],
        weighted[:, :, :, :own_heads],
    )
    high_part = (
        row_peak[:, :, :, own_heads:],
        row_total[:, :, :, own_heads:],
        weighted[:, :, :, own_heads:],
    )
    send_part = tuple(
        (jnp.where(is_even, high_one, low_one) for low_one, high_one in zip(low_part, high_part))
    )
    keep_part = tuple(
        (jnp.where(is_even, low_one, high_one) for low_one, high_one in zip(low_part, high_part))
    )
    got_part = (
        from_partner(send_part[0].astype(jnp.bfloat16), "tp", 0).astype(jnp.float32),
        from_partner(send_part[1].astype(jnp.bfloat16), "tp", 0).astype(jnp.float32),
        from_partner(send_part[2].astype(jnp.bfloat16), "tp", 0).astype(jnp.float32),
    )
    merged_peak = jnp.maximum(keep_part[0], got_part[0])
    own_factor = jnp.exp(keep_part[0] - merged_peak)
    far_factor = jnp.exp(got_part[0] - merged_peak)
    row_total = keep_part[1] * own_factor + got_part[1] * far_factor
    weighted = keep_part[2] * own_factor[..., None] + got_part[2] * far_factor[..., None]
    context = (weighted / row_total[..., None]).astype(jnp.bfloat16).reshape(tokens, -1)
    head_terms = jnp.dot(
        context,
        lax.all_gather(o_weight[0], "grp", axis=1, tiled=True),
        preferred_element_type=jnp.float32,
    )
    result = lax.psum_scatter(
        head_terms.astype(jnp.bfloat16), "tp", scatter_dimension=1, tiled=True
    )
    other_result = from_partner(result, "sec", 0)
    policy_part = jnp.where(sec_place == 0, result, other_result).astype(jnp.float32)
    refer_part = jnp.where(sec_place == 0, other_result, result).astype(jnp.float32)
    local_gap = jnp.sum((policy_part - refer_part) * value_head, axis=1)
    token_gap = lax.psum(local_gap, "tp")
    hidden_out = result.reshape(1, rollouts, new_steps, result.shape[1])
    gap_grid = token_gap.reshape(rollouts, new_steps)
    step_share = new_steps // sec_count
    own_gap = lax.dynamic_slice_in_dim(gap_grid, sec_place * step_share, step_share, 1)
    return (hidden_out, own_gap)


def solution(mesh):
    placed = (
        P("sec", "grp", None, "tp"),
        P("sec", "grp", "tp"),
        P("sec", "grp", "tp"),
        P("sec", "tp", "grp"),
        P("sec", "grp", "tp", None),
        P("grp"),
        P("tp"),
    )
    return jax.shard_map(
        local,
        mesh=mesh,
        in_specs=placed,
        out_specs=(P("sec", "grp", None, "tp"), P("grp", "sec")),
        check_vma=False,
    )
```

profile of v0, /device:TPU:8, one launch (start us, length us, event | category | flops | bytes accessed | tf_op | source)
XLA Modules:
  0.0 563.6 jit_solution(2793352173244113551)
XLA Ops:
  7.2 0.0 all-gather.12.cloned.1.call-start
  7.2 0.7 all-gather.12.cloned.1.call-update
  7.9 0.0 all-gather.8.cloned.1.call-start
  7.9 1.7 reshape_squeeze.6
  9.7 0.0 all-gather.10.cloned.1.call-start
  9.7 0.7 all-gather.10.cloned.1.call-update
  10.4 0.0 all-gather.14.cloned.1.call-start
  10.5 0.5 all-gather.14.cloned.1.call-update
  11.0 0.0 reduce-scatter.2.cloned.1.call-start
  11.1 0.7 broadcast_compare_fusion
  11.8 27.7 %all-gather.12.cloned.1.call-done = bf16[1,8192,128]{2,1,0:T(8,128)(2,1)} async-done(((bf16[1,1024,128]{2,1,0:T(8,128)(2,1)}), bf16[1,8192,128]{2,1,0:T(8,128)(2,1)}) %all-gather.12.cloned.1.call-update) | async-done | bytes 2097168 | tf_op jit(solution)/shard_map/all_gather | solution.py:34
  39.6 109.6 %all-gather.8.cloned.1.call-done = bf16[256,8192]{1,0:T(8,128)(2,1)} async-done(((bf16[256,512]{1,0:T(8,128)(2,1)}), bf16[256,8192]{1,0:T(8,128)(2,1)}) %all-gather.8.cloned.1.call-update) | async-done | bytes 4194320 | tf_op jit(solution)/shard_map/all_gather | solution.py:26
  149.2 4.1 fusion.16
  153.3 0.6 collective-permute-start.1
  154.0 45.2 %all-gather.10.cloned.1.call-done = bf16[1,8192,512]{2,1,0:T(8,128)(2,1)} async-done(((bf16[1,1024,512]{2,1,0:T(8,128)(2,1)}), bf16[1,8192,512]{2,1,0:T(8,128)(2,1)}) %all-gather.10.cloned.1.call-update) | async-done | bytes 8388624 | tf_op jit(solution)/shard_map/all_gather | solution.py:33
  199.1 7.0 %fusion.13 = bf16[256,512]{1,0:T(8,128)(2,1)S(1)} fusion(bf16[256,8192]{1,0:T(8,128)(2,1)} %all-gather.8.cloned.1.call-done, bf16[1,8192,512]{2,1,0:T(8,128)(2,1)} %all-gather.10.cloned.1.call-done), kind=kOutput, calls=%fused_computation.22 | convolution fusion | flops 2147614720 | bytes 12845056 | tf_op jit(solution)/shard_map/dot_general | solution.py:31
  206.1 3.1 collective-permute-start
  209.2 11.7 %copy.9 = bf16[1,64,256,256]{2,3,1,0:T(8,128)(2,1)} copy(bf16[1,64,256,256]{3,2,1,0:T(8,128)(2,1)} %param.11) | data formatting | bytes 16777216 | tf_op args[4]
  221.0 0.1 maximum_bitcast_fusion
  221.0 0.1 copy.19
  221.1 2.4 select_reduce_fusion
  223.6 3.3 fusion.7
  227.0 0.5 fusion.26
  227.5 0.9 bitcast_reduce_fusion
  228.4 0.1 select_convert_fusion.1
  228.5 0.9 collective-permute-start.4
  229.5 0.1 select_convert_fusion.2
  229.6 2.8 collective-permute-start.2
  232.4 1.6 fusion.10
  234.0 0.5 fusion.11
  234.5 0.2 select_convert_fusion
  234.7 1.1 collective-permute-start.3
  235.8 0.1 collective-permute-done.2
  235.9 0.1 fusion.38
  236.0 0.2 fusion.37
  236.2 8.3 %collective-permute-done.3 = bf16[64,4,1,4,128]{4,3,1,0,2:T(4,128)(2,1)S(1)} collective-permute-done((bf16[64,4,1,4,128]{4,3,1,0,2:T(4,128)(2,1)S(1)}, bf16[64,4,1,4,128]{4,3,1,0,2:T(4,128)(2,1)S(1)}, u32[]{:S(2)}, u32[]{:S(2)}) %collective-permute-start.3) | collective-permute-done | bytes 262176 | tf_op jit(solution)/shard_map/ppermute | solution.py:14
  244.5 1.0 fusion.25
  245.4 7.9 %all-gather.14.cloned.1.call-done = bf16[1,512,8192]{2,1,0:T(8,128)(2,1)} async-done(((bf16[1,512,1024]{2,1,0:T(8,128)(2,1)}), bf16[1,512,8192]{2,1,0:T(8,128)(2,1)}) %all-gather.14.cloned.1.call-update) | async-done | bytes 8388624 | tf_op jit(solution)/shard_map/all_gather | solution.py:118
  253.3 7.7 %convolution_convert_fusion = bf16[256,8192]{1,0:T(8,128)(2,1)} fusion(bf16[1,512,8192]{2,1,0:T(8,128)(2,1)} %all-gather.14.cloned.1.call-done, bf16[32,8,4,128]{3,2,1,0:T(4,128)(2,1)S(1)} %bitcast.117), kind=kOutput, calls=%fused_computation | convolution fusion | flops 2149580800 | bytes 12845056 | tf_op jit(solution)/shard_map/dot_general | solution.py:116
  261.1 213.8 %reduce-scatter.2.cloned.1.call-done = bf16[256,512]{1,0:T(8,128)(2,1)} async-done(((bf16[256,8192]{1,0:T(8,128)(2,1)}), bf16[256,512]{1,0:T(8,128)(2,1)}) %reduce-scatter.2.cloned.1.call-update) | async-done | bytes 262160 | tf_op jit(solution)/shard_map/reduce_scatter | solution.py:121
  474.9 0.5 collective-permute-start.5
  475.4 1.8 reshape.158
  477.2 4.3 collective-permute-done.5
  481.5 1.1 multiply_reduce_fusion
  482.6 0.1 reshape.159
  482.7 73.6 %psum.7 = f32[64,4]{1,0:T(8,128)S(1)} all-reduce(f32[64,4]{1,0:T(8,128)S(1)} %reshape.159), channel_id=1, replica_groups=mesh['grp'=8,'tp'=16,'sec'=2] {'tp'}, use_global_device_ids=true, to_apply=%region_6.7 | all-reduce | flops 256 | bytes 2048 | tf_op jit(solution)/shard_map/psum | solution.py:128
  556.3 0.1 constant_dynamic-slice_fusion
  556.4 0.6 copy.12
  (18 shorter events, 0.2 us)
Async XLA Ops:
  7.2 32.4 %all-gather.12.cloned.1.call-start = ((), (), s32[]{:S(2)}) async-start(), calls=%async_computation.4 | async-start | bytes 2359296 | tf_op jit(solution)/shard_map/all_gather | solution.py:34
  7.9 141.3 %all-gather.8.cloned.1.call-start = ((), (), s32[]{:S(2)}) async-start(), calls=%async_computation.1 | async-start | bytes 4456448 | tf_op jit(solution)/shard_map/all_gather | solution.py:26
  9.7 189.4 %all-gather.10.cloned.1.call-start = ((), (), s32[]{:S(2)}) async-start(), calls=%async_computation.3 | async-start | bytes 9437184 | tf_op jit(solution)/shard_map/all_gather | solution.py:33
  10.4 242.9 %all-gather.14.cloned.1.call-start = ((), (), s32[]{:S(2)}) async-start(), calls=%async_computation.5 | async-start | bytes 9437184 | tf_op jit(solution)/shard_map/all_gather | solution.py:118
  11.0 463.9 %reduce-scatter.2.cloned.1.call-start = ((), (), s32[]{:S(2)}) async-start(), calls=%async_computation.2 | async-start | bytes 4456448 | tf_op jit(solution)/shard_map/reduce_scatter | solution.py:121
  153.3 67.6 %collective-permute-start.1 = (bf16[256,128]{1,0:T(8,128)(2,1)S(1)}, bf16[256,128]{1,0:T(8,128)(2,1)S(1)}, u32[]{:S(2)}, u32[]{:S(2)}) collective-permute-start(bf16[256,128]{1,0:T(8,128)(2,1)S(1)} %fusion.16), channel_id=1, source_target_pairs={{0,2},{2,0},{4,6},{6,4},{8,10},{10,8},{12,14},{14,12},{16,18},{18,... | collective-permute-start | bytes 196616 | tf_op jit(solution)/shard_map/ppermute | solution.py:14
  206.1 14.8 %collective-permute-start = (bf16[256,512]{1,0:T(8,128)(2,1)S(1)}, bf16[256,512]{1,0:T(8,128)(2,1)S(1)}, u32[]{:S(2)}, u32[]{:S(2)}) collective-permute-start(bf16[256,512]{1,0:T(8,128)(2,1)S(1)} %fusion.13), channel_id=1, source_target_pairs={{0,2},{2,0},{4,6},{6,4},{8,10},{10,8},{12,14},{14,12},{16,18},{18,... | collective-permute-start | bytes 786440 | tf_op jit(solution)/shard_map/ppermute | solution.py:14
  220.9 11.5 %slice-start = ((s8[8388608]{0:T(1024)(128)(4,1)}), s8[4194304]{0:T(1024)(128)(4,1)S(1)}, s32[]{:S(2)}) async-start(s8[8388608]{0:T(1024)(128)(4,1)} %bitcast.110), calls=%async_computation.6 | async-start | bytes 8388608
  223.6 8.8 %slice-start.1 = ((s8[8388608]{0:T(1024)(128)(4,1)}), s8[4194304]{0:T(1024)(128)(4,1)S(1)}, s32[]{:S(2)}) async-start(s8[8388608]{0:T(1024)(128)(4,1)} %bitcast.110), calls=%async_computation.7 | async-start | bytes 8388608
  228.5 7.5 %collective-permute-start.4 = (bf16[64,4,1,4]{3,1,0,2:T(4,128)(2,1)S(1)}, bf16[64,4,1,4]{3,1,0,2:T(4,128)(2,1)S(1)}, u32[]{:S(2)}, u32[]{:S(2)}) collective-permute-start(bf16[64,4,1,4]{3,1,0,2:T(4,128)(2,1)S(1)} %select_convert_fusion.1), channel_id=1, source_target_pairs={{0,2},{2,0},{4,6},{6,4},{8,10},{10,8},{12,14},{14,12},{16,18},{18,... | collective-permute-start | bytes 6152 | tf_op jit(solution)/shard_map/ppermute | solution.py:14
  229.6 6.3 %collective-permute-start.2 = (bf16[64,4,1,4]{3,1,0,2:T(4,128)(2,1)S(1)}, bf16[64,4,1,4]{3,1,0,2:T(4,128)(2,1)S(1)}, u32[]{:S(2)}, u32[]{:S(2)}) collective-permute-start(bf16[64,4,1,4]{3,1,0,2:T(4,128)(2,1)S(1)} %select_convert_fusion.2), channel_id=1, source_target_pairs={{0,2},{2,0},{4,6},{6,4},{8,10},{10,8},{12,14},{14,12},{16,18},{18,... | collective-permute-start | bytes 6152 | tf_op jit(solution)/shard_map/ppermute | solution.py:14
  234.7 9.8 %collective-permute-start.3 = (bf16[64,4,1,4,128]{4,3,1,0,2:T(4,128)(2,1)S(1)}, bf16[64,4,1,4,128]{4,3,1,0,2:T(4,128)(2,1)S(1)}, u32[]{:S(2)}, u32[]{:S(2)}) collective-permute-start(bf16[64,4,1,4,128]{4,3,1,0,2:T(4,128)(2,1)S(1)} %select_convert_fusion), channel_id=1, source_target_pairs={{0,2},{2,0},{4,6},{6,4},{8,10},{10,8},{12,14},{14,12},{16,18},{18,... | collective-permute-start | bytes 786440 | tf_op jit(solution)/shard_map/ppermute | solution.py:14
  261.0 220.4 %copy-start = (f32[512]{0:T(512)S(1)}, f32[512]{0:T(512)}, u32[]{:S(2)}) copy-start(f32[512]{0:T(512)} %param.13) | copy-start | bytes 6148
  474.9 6.6 %collective-permute-start.5 = (bf16[256,512]{1,0:T(8,128)(2,1)}, bf16[256,512]{1,0:T(8,128)(2,1)S(1)}, u32[]{:S(2)}, u32[]{:S(2)}) collective-permute-start(bf16[256,512]{1,0:T(8,128)(2,1)} %reduce-scatter.2.cloned.1.call-done), channel_id=1, source_target_pairs={{0,1},{1,0},{2,3},{3,2},{4,5},{5,4},{6,7},{7,6},{8,9},{9,8},{10,11... | collective-permute-start | bytes 786440 | tf_op jit(solution)/shard_map/ppermute | solution.py:14
Sparse Core Ops, SparseCore 0:
  9.9 29.6 all-gather.11
  42.6 106.5 all-gather.7
  151.1 48.0 all-gather.9
  200.8 52.4 all-gather.13
  261.2 213.6 reduce-scatter.1
where the time goes:
time: 564 us
  waiting for transfers between devices  419 us (74%)
  blocking collectives  73.6 us (13%)
  matrix products  26.7 us (5%)
  local copies, waits for them, and re-layouts  16.1 us (3%)
  between operations  14 us (2%)
  starting transfers between devices  9.26 us (2%)
    reduce_scatter x1, waiting for transfers between devices, local(): lax.psum_scatter(head_terms.astype(jnp.bfloat16), 'tp', scatter_dimension...  214 us
    all_gather x1, waiting for transfers between devices, local(): full_in = lax.all_gather(local_in, 'tp', axis=1, tiled=True)  110 us
    psum x1, blocking collectives, local(): token_gap = lax.psum(local_gap, 'tp')  73.6 us
    all_gather x1, waiting for transfers between devices, local(): query_sum = add_rows(lax.all_gather(query_local, 'grp', axis=0, tiled=True))  45.2 us
    all_gather x1, waiting for transfers between devices, local(): pair_sum = add_rows(lax.all_gather(pair_local, 'grp', axis=0, tiled=True))  27.7 us
    ppermute x6, waiting for transfers between devices, from_partner(): return lax.ppermute(value, axis, pairs)  12.6 us
    unnamed x9, local copies, waits for them, and re-layouts  12.4 us
  transfers between devices with their start and end apart: 11, of which 8 were waited for; matrix products, arithmetic and copies ran while one was open for 7% of the time, Pallas kernels for 0%

commit v1 on v0

--- a/solution.py
+++ b/solution.py
@@ -125,7 +125,7 @@
     policy_part = jnp.where(sec_place == 0, result, other_result).astype(jnp.float32)
     refer_part = jnp.where(sec_place == 0, other_result, result).astype(jnp.float32)
     local_gap = jnp.sum((policy_part - refer_part) * value_head, axis=1)
-    token_gap = lax.psum(local_gap, "tp")
+    token_gap = jnp.sum(lax.all_gather(local_gap, "tp"), axis=0)
     hidden_out = result.reshape(1, rollouts, new_steps, result.shape[1])
     gap_grid = token_gap.reshape(rollouts, new_steps)
     step_share = new_steps // sec_count

time: 564 us -> 528 us (0.936)
  blocking collectives: 73.6 us -> 37.4 us
    psum x1 -> x0, blocking collectives: 73.6 us -> none  [local(): token_gap = lax.psum(local_gap, 'tp')]
    all_gather x0 -> x1, blocking collectives: none -> 37.4 us  [local(): token_gap = jnp.sum(lax.all_gather(local_gap, 'tp'), axis=0)]
where the time goes in v1:
time: 528 us; the launch traced here: 527 us
  waiting for transfers between devices  419 us (79%)
  blocking collectives  37.4 us (7%)
  matrix products  26.7 us (5%)
  local copies, waits for them, and re-layouts  16.1 us (3%)
  between operations  14 us (3%)
  starting transfers between devices  9.26 us (2%)
    reduce_scatter x1, waiting for transfers between devices, local(): lax.psum_scatter(head_terms.astype(jnp.bfloat16), 'tp', scatter_dimension...  214 us
    all_gather x1, waiting for transfers between devices, local(): full_in = lax.all_gather(local_in, 'tp', axis=1, tiled=True)  110 us
    all_gather x1, waiting for transfers between devices, local(): query_sum = add_rows(lax.all_gather(query_local, 'grp', axis=0, tiled=True))  45.2 us
    all_gather x1, blocking collectives, local(): token_gap = jnp.sum(lax.all_gather(local_gap, 'tp'), axis=0)  37.4 us
    all_gather x1, waiting for transfers between devices, local(): pair_sum = add_rows(lax.all_gather(pair_local, 'grp', axis=0, tiled=True))  27.7 us
    ppermute x6, waiting for transfers between devices, from_partner(): return lax.ppermute(value, axis, pairs)  12.6 us
    unnamed x9, local copies, waits for them, and re-layouts  12.4 us
    dot_general x2, matrix products, add_rows(): return jnp.dot(full_in, piece, preferred_element_type=jnp.float32)  11.1 us
  transfers between devices with their start and end apart: 11, of which 8 were waited for; matrix products, arithmetic and copies ran while one was open for 7% of the time, Pallas kernels for 0%

profile of v1, /device:TPU:8, one launch (start us, length us, event | category | flops | bytes accessed | tf_op | source)
XLA Modules:
  0.0 527.4 jit_solution(1739307713989096729)
XLA Ops:
  7.2 0.0 all-gather.14.cloned.1.call-start
  7.2 0.7 all-gather.14.cloned.1.call-update
  7.9 0.0 all-gather.10.cloned.1.call-start
  7.9 1.7 reshape_squeeze.6
  9.7 0.0 all-gather.12.cloned.1.call-start
  9.7 0.7 all-gather.12.cloned.1.call-update
  10.4 0.0 all-gather.16.cloned.1.call-start
  10.5 0.5 all-gather.16.cloned.1.call-update
  11.0 0.0 reduce-scatter.2.cloned.1.call-start
  11.1 0.7 broadcast_compare_fusion
  11.8 27.7 %all-gather.14.cloned.1.call-done = bf16[1,8192,128]{2,1,0:T(8,128)(2,1)} async-done(((bf16[1,1024,128]{2,1,0:T(8,128)(2,1)}), bf16[1,8192,128]{2,1,0:T(8,128)(2,1)}) %all-gather.14.cloned.1.call-update) | async-done | bytes 2097168 | tf_op jit(solution)/shard_map/all_gather | solution.py:34
  39.6 109.6 %all-gather.10.cloned.1.call-done = bf16[256,8192]{1,0:T(8,128)(2,1)} async-done(((bf16[256,512]{1,0:T(8,128)(2,1)}), bf16[256,8192]{1,0:T(8,128)(2,1)}) %all-gather.10.cloned.1.call-update) | async-done | bytes 4194320 | tf_op jit(solution)/shard_map/all_gather | solution.py:26
  149.2 4.1 fusion.16
  153.3 0.6 collective-permute-start.1
  154.0 45.2 %all-gather.12.cloned.1.call-done = bf16[1,8192,512]{2,1,0:T(8,128)(2,1)} async-done(((bf16[1,1024,512]{2,1,0:T(8,128)(2,1)}), bf16[1,8192,512]{2,1,0:T(8,128)(2,1)}) %all-gather.12.cloned.1.call-update) | async-done | bytes 8388624 | tf_op jit(solution)/shard_map/all_gather | solution.py:33
  199.1 7.0 %fusion.13 = bf16[256,512]{1,0:T(8,128)(2,1)S(1)} fusion(bf16[256,8192]{1,0:T(8,128)(2,1)} %all-gather.10.cloned.1.call-done, bf16[1,8192,512]{2,1,0:T(8,128)(2,1)} %all-gather.12.cloned.1.call-done), kind=kOutput, calls=%fused_computation.22 | convolution fusion | flops 2147614720 | bytes 12845056 | tf_op jit(solution)/shard_map/dot_general | solution.py:31
  206.1 3.1 collective-permute-start
  209.2 11.7 %copy.13 = bf16[1,64,256,256]{2,3,1,0:T(8,128)(2,1)} copy(bf16[1,64,256,256]{3,2,1,0:T(8,128)(2,1)} %param.11) | data formatting | bytes 16777216 | tf_op args[4]
  221.0 0.1 maximum_bitcast_fusion
  221.0 0.1 copy.23
  221.1 2.4 select_reduce_fusion
  223.6 3.3 fusion.7
  227.0 0.5 fusion.26
  227.5 0.9 bitcast_reduce_fusion
  228.4 0.1 select_convert_fusion.1
  228.5 0.9 collective-permute-start.4
  229.5 0.1 select_convert_fusion.2
  229.6 2.8 collective-permute-start.2
  232.4 1.6 fusion.10
  234.0 0.5 fusion.11
  234.5 0.2 select_convert_fusion
  234.7 1.1 collective-permute-start.3
  235.8 0.1 collective-permute-done.2
  235.9 0.1 fusion.38
  236.0 0.2 fusion.37
  236.2 8.3 %collective-permute-done.3 = bf16[64,4,1,4,128]{4,3,1,0,2:T(4,128)(2,1)S(1)} collective-permute-done((bf16[64,4,1,4,128]{4,3,1,0,2:T(4,128)(2,1)S(1)}, bf16[64,4,1,4,128]{4,3,1,0,2:T(4,128)(2,1)S(1)}, u32[]{:S(2)}, u32[]{:S(2)}) %collective-permute-start.3) | collective-permute-done | bytes 262176 | tf_op jit(solution)/shard_map/ppermute | solution.py:14
  244.5 1.0 fusion.25
  245.4 7.9 %all-gather.16.cloned.1.call-done = bf16[1,512,8192]{2,1,0:T(8,128)(2,1)} async-done(((bf16[1,512,1024]{2,1,0:T(8,128)(2,1)}), bf16[1,512,8192]{2,1,0:T(8,128)(2,1)}) %all-gather.16.cloned.1.call-update) | async-done | bytes 8388624 | tf_op jit(solution)/shard_map/all_gather | solution.py:118
  253.3 7.7 %convolution_convert_fusion = bf16[256,8192]{1,0:T(8,128)(2,1)} fusion(bf16[1,512,8192]{2,1,0:T(8,128)(2,1)} %all-gather.16.cloned.1.call-done, bf16[32,8,4,128]{3,2,1,0:T(4,128)(2,1)S(1)} %bitcast.118), kind=kOutput, calls=%fused_computation | convolution fusion | flops 2149580800 | bytes 12845056 | tf_op jit(solution)/shard_map/dot_general | solution.py:116
  261.1 213.8 %reduce-scatter.2.cloned.1.call-done = bf16[256,512]{1,0:T(8,128)(2,1)} async-done(((bf16[256,8192]{1,0:T(8,128)(2,1)}), bf16[256,512]{1,0:T(8,128)(2,1)}) %reduce-scatter.2.cloned.1.call-update) | async-done | bytes 262160 | tf_op jit(solution)/shard_map/reduce_scatter | solution.py:121
  474.9 0.5 collective-permute-start.5
  475.4 1.8 reshape.158
  477.2 4.3 collective-permute-done.5
  481.5 1.1 multiply_reduce_fusion
  482.6 37.4 %all-gather.4 = f32[16,1,256]{2,1,0:T(1,128)S(1)} all-gather(f32[1,1,256]{2,1,0:T(1,128)S(1)} %bitcast.121), channel_id=5, replica_groups=mesh['grp'=8,'tp'=16,'sec'=2] {'tp'}, dimensions={0}, use_global_device_ids=true | all-gather | bytes 17408 | tf_op jit(solution)/shard_map/all_gather | solution.py:128
  520.0 0.1 reshape.159
  520.1 0.1 constant_dynamic-slice_fusion
  520.2 0.6 copy.16
  (19 shorter events, 0.2 us)
Async XLA Ops:
  7.2 32.4 %all-gather.14.cloned.1.call-start = ((), (), s32[]{:S(2)}) async-start(), calls=%async_computation.4 | async-start | bytes 2359296 | tf_op jit(solution)/shard_map/all_gather | solution.py:34
  7.9 141.3 %all-gather.10.cloned.1.call-start = ((), (), s32[]{:S(2)}) async-start(), calls=%async_computation.1 | async-start | bytes 4456448 | tf_op jit(solution)/shard_map/all_gather | solution.py:26
  9.7 189.4 %all-gather.12.cloned.1.call-start = ((), (), s32[]{:S(2)}) async-start(), calls=%async_computation.3 | async-start | bytes 9437184 | tf_op jit(solution)/shard_map/all_gather | solution.py:33
  10.4 242.9 %all-gather.16.cloned.1.call-start = ((), (), s32[]{:S(2)}) async-start(), calls=%async_computation.5 | async-start | bytes 9437184 | tf_op jit(solution)/shard_map/all_gather | solution.py:118
  11.0 463.9 %reduce-scatter.2.cloned.1.call-start = ((), (), s32[]{:S(2)}) async-start(), calls=%async_computation.2 | async-start | bytes 4456448 | tf_op jit(solution)/shard_map/reduce_scatter | solution.py:121
  153.3 67.6 %collective-permute-start.1 = (bf16[256,128]{1,0:T(8,128)(2,1)S(1)}, bf16[256,128]{1,0:T(8,128)(2,1)S(1)}, u32[]{:S(2)}, u32[]{:S(2)}) collective-permute-start(bf16[256,128]{1,0:T(8,128)(2,1)S(1)} %fusion.16), channel_id=1, source_target_pairs={{0,2},{2,0},{4,6},{6,4},{8,10},{10,8},{12,14},{14,12},{16,18},{18,... | collective-permute-start | bytes 196616 | tf_op jit(solution)/shard_map/ppermute | solution.py:14
  206.1 14.8 %collective-permute-start = (bf16[256,512]{1,0:T(8,128)(2,1)S(1)}, bf16[256,512]{1,0:T(8,128)(2,1)S(1)}, u32[]{:S(2)}, u32[]{:S(2)}) collective-permute-start(bf16[256,512]{1,0:T(8,128)(2,1)S(1)} %fusion.13), channel_id=1, source_target_pairs={{0,2},{2,0},{4,6},{6,4},{8,10},{10,8},{12,14},{14,12},{16,18},{18,... | collective-permute-start | bytes 786440 | tf_op jit(solution)/shard_map/ppermute | solution.py:14
  220.9 11.5 %slice-start = ((s8[8388608]{0:T(1024)(128)(4,1)}), s8[4194304]{0:T(1024)(128)(4,1)S(1)}, s32[]{:S(2)}) async-start(s8[8388608]{0:T(1024)(128)(4,1)} %bitcast.111), calls=%async_computation.6 | async-start | bytes 8388608
  223.6 8.8 %slice-start.1 = ((s8[8388608]{0:T(1024)(128)(4,1)}), s8[4194304]{0:T(1024)(128)(4,1)S(1)}, s32[]{:S(2)}) async-start(s8[8388608]{0:T(1024)(128)(4,1)} %bitcast.111), calls=%async_computation.7 | async-start | bytes 8388608
  228.5 7.5 %collective-permute-start.4 = (bf16[64,4,1,4]{3,1,0,2:T(4,128)(2,1)S(1)}, bf16[64,4,1,4]{3,1,0,2:T(4,128)(2,1)S(1)}, u32[]{:S(2)}, u32[]{:S(2)}) collective-permute-start(bf16[64,4,1,4]{3,1,0,2:T(4,128)(2,1)S(1)} %select_convert_fusion.1), channel_id=1, source_target_pairs={{0,2},{2,0},{4,6},{6,4},{8,10},{10,8},{12,14},{14,12},{16,18},{18,... | collective-permute-start | bytes 6152 | tf_op jit(solution)/shard_map/ppermute | solution.py:14
  229.6 6.3 %collective-permute-start.2 = (bf16[64,4,1,4]{3,1,0,2:T(4,128)(2,1)S(1)}, bf16[64,4,1,4]{3,1,0,2:T(4,128)(2,1)S(1)}, u32[]{:S(2)}, u32[]{:S(2)}) collective-permute-start(bf16[64,4,1,4]{3,1,0,2:T(4,128)(2,1)S(1)} %select_convert_fusion.2), channel_id=1, source_target_pairs={{0,2},{2,0},{4,6},{6,4},{8,10},{10,8},{12,14},{14,12},{16,18},{18,... | collective-permute-start | bytes 6152 | tf_op jit(solution)/shard_map/ppermute | solution.py:14
  234.7 9.8 %collective-permute-start.3 = (bf16[64,4,1,4,128]{4,3,1,0,2:T(4,128)(2,1)S(1)}, bf16[64,4,1,4,128]{4,3,1,0,2:T(4,128)(2,1)S(1)}, u32[]{:S(2)}, u32[]{:S(2)}) collective-permute-start(bf16[64,4,1,4,128]{4,3,1,0,2:T(4,128)(2,1)S(1)} %select_convert_fusion), channel_id=1, source_target_pairs={{0,2},{2,0},{4,6},{6,4},{8,10},{10,8},{12,14},{14,12},{16,18},{18,... | collective-permute-start | bytes 786440 | tf_op jit(solution)/shard_map/ppermute | solution.py:14
  261.0 220.4 %copy-start = (f32[512]{0:T(512)S(1)}, f32[512]{0:T(512)}, u32[]{:S(2)}) copy-start(f32[512]{0:T(512)} %param.13) | copy-start | bytes 6148
  474.9 6.6 %collective-permute-start.5 = (bf16[256,512]{1,0:T(8,128)(2,1)}, bf16[256,512]{1,0:T(8,128)(2,1)S(1)}, u32[]{:S(2)}, u32[]{:S(2)}) collective-permute-start(bf16[256,512]{1,0:T(8,128)(2,1)} %reduce-scatter.2.cloned.1.call-done), channel_id=1, source_target_pairs={{0,1},{1,0},{2,3},{3,2},{4,5},{5,4},{6,7},{7,6},{8,9},{9,8},{10,11... | collective-permute-start | bytes 786440 | tf_op jit(solution)/shard_map/ppermute | solution.py:14
Sparse Core Ops, SparseCore 0:
  9.9 29.6 all-gather.13
  42.6 106.5 all-gather.9
  151.1 48.0 all-gather.11
  200.8 52.4 all-gather.15
  261.2 213.6 reduce-scatter.1
